TPU v7x, 1024 devices: a whole 4x8x16 slice. The times are simulated.
1024 devices in a mesh: dp: 32 (over z_hi, y, core), group: 32 (over x, z_lo).
Axes of the slice: x: 4, y: 8, z: 16 (z_hi: 2, z_lo: 8; z = z_hi * 8 + z_lo), core: 2. Of those that a mesh axis runs over, the one named last changes fastest.
Arguments:
- image_embeds: bfloat16 [16384, 1152], P('dp'), may hold values from -0.1796875 to 0.1796875
- text_embeds: bfloat16 [16384, 1152], P(('dp', 'group')), may hold values from -0.1796875 to 0.1796875
- scale_logarithm: float32 [1], replicated, may hold values from 1.6 to 2.6
- logit_bias: float32 [1], replicated, may hold values from -6 to -2
Outputs:
- image_grads: float32 [16384, 1152], P(('dp', 'group'))
- text_grads: float32 [16384, 1152], P(('dp', 'group'))
All inputs are finite; a program needn't handle non-finite values.
Results may differ from a plain program's by a relative error of at most 0.004.
Values may be sent and summed in bfloat16 or wider, within the bound.
A program may use at most 32 MiB of HBM per device.

v0:
```python
import jax
import jax.numpy as jnp
from jax import lax
from jax.sharding import PartitionSpec as P


def normalize(embeds):
    values = embeds.astype(jnp.float32)
    inverse_norm = lax.rsqrt(jnp.sum(values * values, axis=1, keepdims=True) + 1e-06)
    return (values * inverse_norm, inverse_norm)


def norm_backward(unit_rows, unit_grad, inverse_norm):
    along = jnp.sum(unit_rows * unit_grad, axis=1, keepdims=True)
    return (unit_grad - unit_rows * along) * inverse_norm


def body(image_embeds, text_embeds, scale_logarithm, logit_bias):
    scale_factor = jnp.exp(scale_logarithm[0])
    shift_amount = logit_bias[0]
    row_count = text_embeds.shape[0]
    block_rows = image_embeds.shape[0]
    cycle_place = lax.axis_index("dp")
    group_place = lax.axis_index("group")
    image_unit, image_norm = normalize(image_embeds)
    text_unit, text_norm = normalize(text_embeds)
    image_half = image_unit.astype(jnp.bfloat16)
    text_second_half = text_unit.astype(jnp.bfloat16)
    image_ids = cycle_place * block_rows + jnp.arange(block_rows, dtype=jnp.int32)
    collected_rows = lax.all_gather(text_second_half, "dp", axis=0, tiled=True)
    row_blocks = jnp.arange(collected_rows.shape[0], dtype=jnp.int32) // row_count
    inner = jnp.arange(collected_rows.shape[0], dtype=jnp.int32) % row_count
    text_ids = row_blocks * block_rows + group_place * row_count + inner
    similarity_matrix = lax.dot_general(
        image_half, collected_rows, (((1,), (1,)), ((), ())), preferred_element_type=jnp.float32
    )
    pair_logits = scale_factor * similarity_matrix + shift_amount
    label_sign = jnp.where(
        image_ids[:, None] == text_ids[None, :], jnp.float32(1.0), jnp.float32(-1.0)
    )
    loss_factor = (-label_sign * jax.nn.sigmoid(-label_sign * pair_logits)).astype(jnp.bfloat16)
    image_gradient_total = scale_factor * jnp.dot(
        loss_factor, collected_rows, preferred_element_type=jnp.float32
    )
    text_unit_grad = lax.psum_scatter(
        scale_factor
        * lax.dot_general(
            loss_factor, image_half, (((0,), (0,)), ((), ())), preferred_element_type=jnp.float32
        ),
        "dp",
        scatter_dimension=0,
        tiled=True,
    )
    image_unit_grad = lax.psum_scatter(
        image_gradient_total, "group", scatter_dimension=0, tiled=True
    )
    own_unit = lax.dynamic_slice_in_dim(image_unit, group_place * row_count, row_count, 0)
    own_norm = lax.dynamic_slice_in_dim(image_norm, group_place * row_count, row_count, 0)
    image_grads = norm_backward(own_unit, image_unit_grad, own_norm)
    text_grads = norm_backward(text_unit, text_unit_grad, text_norm)
    return (image_grads, text_grads)


def solution(mesh):
    return jax.shard_map(
        body,
        mesh=mesh,
        in_specs=(P("dp", None), P(("dp", "group"), None), P(), P()),
        out_specs=(P(("dp", "group"), None), P(("dp", "group"), None)),
        check_vma=False,
    )
```

profile of v0, /device:TPU:8, one launch (start us, length us, event | category | flops | bytes accessed | tf_op | source)
XLA Modules:
  0.0 553.9 jit_solution(6880101169742424826)
XLA Ops:
  7.2 0.0 all-gather.2.cloned.1.call-start
  7.2 0.9 fusion.17
  8.1 1.5 fusion.13
  9.6 0.0 all-gather.2.cloned.1.call-update
  9.6 0.0 reduce-scatter.5.cloned.1.call-start
  11.0 1.6 fusion
  12.6 119.3 %all-gather.2.cloned.1.call-done = bf16[512,1152]{1,0:T(8,128)(2,1)} async-done(((bf16[16,1152]{1,0:T(8,128)(2,1)}), bf16[512,1152]{1,0:T(8,128)(2,1)}) %all-gather.2.cloned.1.call-update) | async-done | bytes 1179664 | tf_op jit(solution)/shard_map/all_gather | solution.py:30
  131.9 0.0 copy-start
  131.9 2.9 fusion.8
  134.8 0.0 copy-done
  134.8 0.0 copy-start.1
  134.8 2.4 convolution_multiply_fusion
  137.2 0.0 reduce-scatter.5.cloned.1.call-update
  137.2 0.0 reduce-scatter.3.cloned.1.call-start
  137.3 0.0 copy-done.1
  137.3 2.2 convolution_multiply_fusion.1
  139.5 0.0 reduce-scatter.3.cloned.1.call-update
  139.5 0.1 dynamic-slice.3
  139.6 0.2 convert_multiply_fusion
  139.8 159.5 %reduce-scatter.5.cloned.1.call-done = f32[16,1152]{1,0:T(8,128)} async-done(((f32[512,1152]{1,0:T(8,128)}), f32[16,1152]{1,0:T(8,128)}) %reduce-scatter.5.cloned.1.call-update) | async-done | bytes 73744 | tf_op jit(solution)/shard_map/reduce_scatter | solution.py:45
  299.3 1.1 fusion.14
  300.4 1.6 fusion.16
  302.0 242.7 %reduce-scatter.3.cloned.1.call-done = f32[16,1152]{1,0:T(8,128)} async-done(((f32[512,1152]{1,0:T(8,128)}), f32[16,1152]{1,0:T(8,128)}) %reduce-scatter.3.cloned.1.call-update) | async-done | bytes 73744 | tf_op jit(solution)/shard_map/reduce_scatter | solution.py:54
  544.7 1.0 multiply_reduce_fusion
  545.7 1.6 subtract_multiply_fusion
  (3 shorter events, 0.0 us)
Async XLA Ops:
  7.2 124.7 %all-gather.2.cloned.1.call-start = ((), (), s32[]{:S(2)}) async-start(), calls=%async_computation.2 | async-start | bytes 1216512 | tf_op jit(solution)/shard_map/all_gather | solution.py:30
  9.6 289.7 %reduce-scatter.5.cloned.1.call-start = ((), (), s32[]{:S(2)}) async-start(), calls=%async_computation.4 | async-start | bytes 2433024 | tf_op jit(solution)/shard_map/reduce_scatter | solution.py:45
  131.9 2.9 copy-start
  134.8 2.4 copy-start.1
  137.2 407.5 %reduce-scatter.3.cloned.1.call-start = ((), (), s32[]{:S(2)}) async-start(), calls=%async_computation.3 | async-start | bytes 2433024 | tf_op jit(solution)/shard_map/reduce_scatter | solution.py:54
Sparse Core Ops, SparseCore 0:
  13.0 118.9 all-gather.1
  137.8 161.4 reduce-scatter.4
  302.7 241.9 reduce-scatter.2
where the time goes:
time: 554 us
  waiting for transfers between devices  522 us (94%)
  between operations  15.1 us (3%)
  other arithmetic  9.46 us (2%)
  matrix products  7.48 us (1%)
    reduce_scatter x1, waiting for transfers between devices, body(): lax.psum_scatter(image_gradient_total, 'group', scatter_dimension=0, tile...  243 us
    reduce_scatter x1, waiting for transfers between devices, body(): lax.psum_scatter(scale_factor * lax.dot_general(loss_factor, image_half,...  159 us
    all_gather x1, waiting for transfers between devices, body(): collected_rows = lax.all_gather(text_second_half, 'dp', axis=0, tiled=True)  119 us
  transfers between devices with their start and end apart: 3, of which 3 were waited for; matrix products, arithmetic and copies ran while one was open for 1% of the time, Pallas kernels for 0%

commit v1 on v0

v1 whole, which is shorter than its diff:
```python
import jax
import jax.numpy as jnp
from jax import lax
from jax.experimental import pallas as pl
from jax.experimental.pallas import tpu as pltpu
from jax.sharding import PartitionSpec as P

NX = 4
NY = 8
NZ = 8
ROWS = 16

def offsets(count):
    found = [0]
    for distance in range(1, count // 2 + 1):
        found += [distance, -distance]
    return found[:count]


def inverse_norms(values):
    return lax.rsqrt(jnp.sum(values * values, axis=1, keepdims=True) + 1e-06)


def norm_backward(unit_rows, unit_grad, inverse_norm):
    along = jnp.sum(unit_rows * unit_grad, axis=1, keepdims=True)
    return (unit_grad - unit_rows * along) * inverse_norm


def kernel(
    image_hbm, text_ref, scale_ref, bias_ref, image_out, text_out,
    image_in, image_half, texts, coef, coef_text,
    pair_send, pair_recv, text_own, y_send, y_recv, hi_send, hi_recv,
    x_own, x_send, x_recv, z_own, z_send, z_recv,
    in_sem, gather_recv, gather_pair_recv, pair_sem, y_sem, hi_sem, x_sem, z_sem, send_sems,
):
    dp = lax.axis_index("dp")
    group = lax.axis_index("group")
    core = lax.rem(dp, 2)
    y = lax.rem(dp // 2, NY)
    z_hi = dp // (2 * NY)
    x = group // NZ
    z_lo = lax.rem(group, NZ)
    moves = offsets(NY)
    pair_rows = 2 * ROWS
    x_rows = NZ * ROWS

    def dp_at(z_hi, y, core):
        return (z_hi * NY + y) * 2 + core

    sibling = (dp_at(z_hi, y, 1 - core), group)
    opposite = (dp_at(1 - z_hi, y, core), group)

    def y_peer(move):
        return (dp_at(z_hi, lax.rem(y + move + NY, NY), core), group)

    def x_peer(k):
        return (dp, lax.rem(x + k, NX) * NZ + z_lo)

    def z_peer(k):
        return (dp, x * NZ + lax.rem(z_lo + k, NZ))

    load = pltpu.make_async_copy(image_hbm, image_in, in_sem)
    load.start()

    peers = [sibling, opposite]
    peers += [y_peer(move) for move in moves[1:]]
    peers += [x_peer(k) for k in range(1, NX)]
    peers += [z_peer(k) for k in range(1, NZ)]
    barrier = pltpu.get_barrier_semaphore()
    for peer in peers:
        pl.semaphore_signal(barrier, inc=1, device_id=peer, device_id_type=pl.DeviceIdType.MESH)

    text_values = text_ref[...].astype(jnp.float32)
    text_norm = inverse_norms(text_values)
    texts[pl.ds(0, ROWS), :] = (text_values * text_norm).astype(jnp.bfloat16)
    pl.semaphore_wait(barrier, len(peers))

    sent = []

    def send(source, target, arrival, device):
        copy = pltpu.make_async_remote_copy(
            src_ref=source, dst_ref=target, send_sem=send_sems.at[len(sent)], recv_sem=arrival,
            device_id=device, device_id_type=pl.DeviceIdType.MESH,
        )
        copy.start()
        sent.append(copy)
        return copy

    def arrived(target, arrival):
        pltpu.make_async_copy(target, target, arrival).wait()

    def place(p, s, r, count=ROWS):
        return texts.at[pl.ds(p * 4 * ROWS + s * pair_rows + r * ROWS, count), :]

    send(place(0, 0, 0), place(0, 0, 1), gather_recv.at[0, 1], opposite)
    for p in range(NY - 1, 0, -1):
        send(place(0, 0, 0), place(p, 0, 0), gather_recv.at[p, 0], y_peer(moves[p]))
    send(place(0, 0, 0), place(0, 1, 0), gather_pair_recv.at[0, 0], sibling)

    load.wait()

    @pl.loop(0, NX)
    def _(i):
        rows = pl.ds(pl.multiple_of(i * x_rows, x_rows), x_rows)
        values = image_in[rows, :].astype(jnp.float32)
        image_half[rows, :] = (values * inverse_norms(values)).astype(jnp.bfloat16)

    scale_row = jnp.exp(jnp.full((1, image_half.shape[0]), scale_ref[0], jnp.float32))
    bias = bias_ref[0]

    def coefficients(chunk, count):
        start = chunk * count
        logits = lax.dot_general(
            texts[pl.ds(start, count), :], image_half[...], (((1,), (1,)), ((), ())),
            preferred_element_type=jnp.float32,
        ) * scale_row + bias
        if chunk == 0:
            text_ids = lax.broadcasted_iota(jnp.int32, logits.shape, 0)
            image_ids = lax.broadcasted_iota(jnp.int32, logits.shape, 1)
            same = jnp.logical_and(text_ids < ROWS, image_ids == text_ids + group * ROWS)
            sign = jnp.where(same, jnp.float32(1.0), jnp.float32(-1.0))
            values = -sign / (1.0 + jnp.exp(sign * logits))
        else:
            values = 1.0 / (1.0 + jnp.exp(-logits))
        coef_text[pl.ds(start, count), :] = values.astype(jnp.bfloat16)
        coef[:, pl.ds(start, count)] = values.T.astype(jnp.bfloat16)

    arrived(place(0, 0, 1), gather_recv.at[0, 1])
    for p in range(NY - 1, 0, -1):
        send(place(0, 0, 1), place(p, 0, 1), gather_recv.at[p, 1], y_peer(moves[p]))
    send(place(0, 0, 1), place(0, 1, 1), gather_pair_recv.at[0, 1], sibling)

    def take(p):
        if p > 0:
            arrived(place(p, 0, 0), gather_recv.at[p, 0])
            arrived(place(p, 0, 1), gather_recv.at[p, 1])
            send(place(p, 0, 0, pair_rows), place(p, 1, 0, pair_rows), gather_pair_recv.at[p, 0], sibling)

    def take_pair(p):
        if p > 0:
            arrived(place(p, 1, 0, pair_rows), gather_pair_recv.at[p, 0])
        else:
            arrived(place(0, 1, 0), gather_pair_recv.at[0, 0])
            arrived(place(0, 1, 1), gather_pair_recv.at[0, 1])

    chunks = NY // 2
    chunk_rows = 2 * 4 * ROWS
    for chunk in range(chunks + 1):
        if chunk < chunks:
            take(2 * chunk)
            take(2 * chunk + 1)
        if chunk > 0:
            take_pair(2 * chunk - 2)
            take_pair(2 * chunk - 1)
            coefficients(chunk - 1, chunk_rows)

    for k in [2, 1, 3, 0] if NX == 4 else [1, 0]:
        rows = pl.ds(pl.multiple_of(lax.rem(x + k, NX) * x_rows, x_rows), x_rows)
        share = jnp.dot(coef[rows, :], texts[...], preferred_element_type=jnp.float32)
        if k == 0:
            x_own[...] = share
        else:
            x_send[k] = share.astype(jnp.bfloat16)
            send(x_send.at[k], x_recv.at[k], x_sem.at[k], x_peer(k))

    for chunk in range(chunks - 1, -1, -1):
        share = jnp.dot(
            coef_text[pl.ds(chunk * chunk_rows, chunk_rows), :], image_half[...],
            preferred_element_type=jnp.float32,
        )
        for half in range(2):
            p = 2 * chunk + half
            base = half * 4 * ROWS
            text_own[p] = share[base : base + pair_rows]
            pair_send[p] = share[base + pair_rows : base + 2 * pair_rows].astype(jnp.bfloat16)
            send(pair_send.at[p], pair_recv.at[p], pair_sem.at[p], sibling)
    for p in range(NY - 1, -1, -1):
        arrived(pair_recv.at[p], pair_sem.at[p])
        both = text_own[p] + pair_recv[p].astype(jnp.float32)
        if p == 0:
            text_own[0] = both
        else:
            y_send[p] = both.astype(jnp.bfloat16)
            send(y_send.at[p], y_recv.at[p], y_sem.at[p], y_peer(-moves[p]))

    for k in range(1, NX):
        arrived(x_recv.at[k], x_sem.at[k])
    for k in list(range(1, NZ)) + [0]:
        rows = pl.ds(pl.multiple_of(lax.rem(z_lo + k, NZ) * ROWS, ROWS), ROWS)
        total = x_own[rows, :]
        for i in range(1, NX):
            total += x_recv[i, rows, :].astype(jnp.float32)
        if k == 0:
            z_own[...] = total
        else:
            z_send[k] = total.astype(jnp.bfloat16)
            send(z_send.at[k], z_recv.at[k], z_sem.at[k], z_peer(k))

    total = text_own[0]
    for p in range(1, NY):
        arrived(y_recv.at[p], y_sem.at[p])
        total += y_recv[p].astype(jnp.float32)
    hi_send[...] = total[ROWS:].astype(jnp.bfloat16)
    send(hi_send, hi_recv, hi_sem, opposite)
    text_total = total[:ROWS]

    scale = jnp.exp(jnp.full((1, image_in.shape[1]), scale_ref[0], jnp.float32))
    total = z_own[...]
    for k in range(1, NZ):
        arrived(z_recv.at[k], z_sem.at[k])
        total += z_recv[k].astype(jnp.float32)
    own = image_in[pl.ds(pl.multiple_of(group * ROWS, ROWS), ROWS), :].astype(jnp.float32)
    own_norm = inverse_norms(own)
    image_out[...] = norm_backward(own * own_norm, total * scale, own_norm)

    arrived(hi_recv, hi_sem)
    text_total += hi_recv[...].astype(jnp.float32)
    text_out[...] = norm_backward(text_values * text_norm, text_total * scale, text_norm)

    for copy in sent:
        copy.wait_send()


def body(image_embeds, text_embeds, scale_logarithm, logit_bias):
    images, width = image_embeds.shape
    count = NY * 4 * ROWS
    x_rows = NZ * ROWS
    sends = 2 * NY + 1 + NY - 1 + NX - 1 + 2 * NY - 1 + NZ - 1 + 1 + 2
    half = jnp.bfloat16
    dma = pltpu.SemaphoreType.DMA
    return pl.pallas_call(
        kernel,
        out_shape=[jax.ShapeDtypeStruct((ROWS, width), jnp.float32)] * 2,
        in_specs=[
            pl.BlockSpec(memory_space=pl.ANY),
            pl.BlockSpec(memory_space=pltpu.VMEM),
            pl.BlockSpec(memory_space=pltpu.SMEM),
            pl.BlockSpec(memory_space=pltpu.SMEM),
        ],
        out_specs=[pl.BlockSpec(memory_space=pltpu.VMEM)] * 2,
        scratch_shapes=[
            pltpu.VMEM((images, width), half),
            pltpu.VMEM((images, width), half),
            pltpu.VMEM((count, width), half),
            pltpu.VMEM((images, count), half),
            pltpu.VMEM((count, images), half),
            pltpu.VMEM((NY, 2 * ROWS, width), half),
            pltpu.VMEM((NY, 2 * ROWS, width), half),
            pltpu.VMEM((NY, 2 * ROWS, width), jnp.float32),
            pltpu.VMEM((NY, 2 * ROWS, width), half),
            pltpu.VMEM((NY, 2 * ROWS, width), half),
            pltpu.VMEM((ROWS, width), half),
            pltpu.VMEM((ROWS, width), half),
            pltpu.VMEM((x_rows, width), jnp.float32),
            pltpu.VMEM((NX, x_rows, width), half),
            pltpu.VMEM((NX, x_rows, width), half),
            pltpu.VMEM((ROWS, width), jnp.float32),
            pltpu.VMEM((NZ, ROWS, width), half),
            pltpu.VMEM((NZ, ROWS, width), half),
            dma,
            dma((NY, 2)),
            dma((NY, 2)),
            dma((NY,)),
            dma((NY,)),
            dma,
            dma((NX,)),
            dma((NZ,)),
            dma((sends,)),
        ],
        compiler_params=pltpu.CompilerParams(
            collective_id=0, has_side_effects=True, vmem_limit_bytes=48 * 1024 * 1024
        ),
        cost_estimate=pl.CostEstimate(
            flops=6 * images * count * width, bytes_accessed=4 * images * width,
            transcendentals=images * count,
        ),
    )(image_embeds, text_embeds, scale_logarithm, logit_bias)


def solution(mesh):
    return jax.shard_map(
        body,
        mesh=mesh,
        in_specs=(P("dp", None), P(("dp", "group"), None), P(), P()),
        out_specs=(P(("dp", "group"), None), P(("dp", "group"), None)),
        check_vma=False,
    )
```

time: 554 us -> 83.5 us (0.15)
  the two profiles are of different devices: /device:TPU:8 before, /device:TPU:128 now
where the time goes in v1:
time: 83.5 us; the launch traced here: 83.2 us
  Pallas kernels  78 us (93%)
  local copies, waits for them, and re-layouts  3.3 us (4%)
  between operations  1.94 us (2%)
    pallas_call x1, Pallas kernels, body(): pl.pallas_call(kernel, out_shape=[jax.ShapeDtypeStruct((ROWS, width), jnp...  78 us
    unnamed x6, local copies, waits for them, and re-layouts  3.3 us

profile of v1, /device:TPU:128, one launch (start us, length us, event | category | flops | bytes accessed | tf_op | source)
XLA Modules:
  0.0 83.2 jit_solution(1345561093157223503)
XLA Ops:
  1.9 0.0 copy-start
  1.9 1.3 %copy-done = bf16[512,1152]{1,0:T(8,128)(2,1)S(1)} copy-done((bf16[512,1152]{1,0:T(8,128)(2,1)S(1)}, bf16[512,1152]{1,0:T(8,128)(2,1)}, u32[]{:S(2)}) %copy-start) | copy-done | bytes 1179672
  3.2 0.0 copy-start.1
  3.2 0.8 copy-done.1
  4.0 78.0 %shard_map.59 = (f32[16,1152]{1,0:T(8,128)S(1)}, f32[16,1152]{1,0:T(8,128)S(1)}) custom-call(bf16[512,1152]{1,0:T(8,128)(2,1)S(1)} %copy-done, bf16[16,1152]{1,0:T(8,128)(2,1)S(1)} %copy-done.1, f32[1]{0:T(128)S(6)} %copy.8.scale_ref, f32[1]{0:T(128)S(6)} %copy.9.bias_ref), custom_call_target="tpu_custom_call" | custom-call | flops 1811939328 | bytes 2359296 | tf_op jit(solution)/shard_map/pallas_call | solution.py:231
  81.9 0.6 copy.10
  82.6 0.6 copy.11
Async XLA Ops:
  1.9 1.3 %copy-start = (bf16[512,1152]{1,0:T(8,128)(2,1)S(1)}, bf16[512,1152]{1,0:T(8,128)(2,1)}, u32[]{:S(2)}) copy-start(bf16[512,1152]{1,0:T(8,128)(2,1)} %image_hbm.1) | copy-start | bytes 3538948
  3.2 0.8 copy-start.1

commit v2 on v1

v2 whole, which is shorter than its diff:
```python
import jax
import jax.numpy as jnp
from jax import lax
from jax.experimental import pallas as pl
from jax.experimental.pallas import tpu as pltpu
from jax.sharding import PartitionSpec as P

NX = 4
NY = 8
NZ = 8
ROWS = 16
VMEM_BYTES = 56 * 1024 * 1024

def offsets(count):
    found = [0]
    for distance in range(1, count // 2 + 1):
        found += [distance, -distance]
    return found[:count]


def inverse_norms(values):
    return lax.rsqrt(jnp.sum(values * values, axis=1, keepdims=True) + 1e-06)


def norm_backward(unit_rows, unit_grad, inverse_norm):
    along = jnp.sum(unit_rows * unit_grad, axis=1, keepdims=True)
    return (unit_grad - unit_rows * along) * inverse_norm


def kernel(
    image_hbm, text_hbm, scale_hbm, bias_hbm, image_out, text_out,
    image_in, text_in, scale_in, bias_in, image_half, texts, coef, coef_text,
    pair_send, pair_recv, text_own, y_send, y_recv, hi_send, hi_recv,
    x_own, x_send, x_recv, z_own, near_send, near_recv, far_send, far_recv,
    in_sems, gather_recv, gather_pair_recv, pair_sem, y_sem, hi_sem, x_sem, near_sem, far_sem,
    send_sems,
):
    dp = lax.axis_index("dp")
    group = lax.axis_index("group")
    core = lax.rem(dp, 2)
    y = lax.rem(dp // 2, NY)
    z_hi = dp // (2 * NY)
    x = group // NZ
    z_lo = lax.rem(group, NZ)
    z_pair = z_lo // 2
    z_side = lax.rem(z_lo, 2)
    moves = offsets(NY)
    pairs = NZ // 2
    x_rows = NZ * ROWS
    pair_rows = 2 * ROWS

    def dp_at(z_hi, y, core):
        return (z_hi * NY + y) * 2 + core

    sibling = (dp_at(z_hi, y, 1 - core), group)
    opposite = (dp_at(1 - z_hi, y, core), group)
    near = (dp, x * NZ + z_pair * 2 + 1 - z_side)

    def y_peer(move):
        return (dp_at(z_hi, lax.rem(y + move + NY, NY), core), group)

    def x_peer(k):
        return (dp, lax.rem(x + k, NX) * NZ + z_lo)

    def far_peer(j):
        return (dp, x * NZ + lax.rem(z_pair + j, pairs) * 2 + z_side)

    loads = [
        pltpu.make_async_copy(source, target, in_sems.at[i])
        for i, (source, target) in enumerate(
            [(text_hbm, text_in), (image_hbm, image_in), (scale_hbm, scale_in), (bias_hbm, bias_in)]
        )
    ]
    for load in loads:
        load.start()

    peers = [opposite, sibling, near]
    peers += [y_peer(move) for move in moves[1:]]
    peers += [x_peer(k) for k in range(1, NX)]
    peers += [far_peer(j) for j in range(1, pairs)]
    barrier = pltpu.get_barrier_semaphore()
    for peer in peers:
        pl.semaphore_signal(barrier, inc=1, device_id=peer, device_id_type=pl.DeviceIdType.MESH)

    loads[0].wait()
    text_values = text_in[...].astype(jnp.float32)
    text_norm = inverse_norms(text_values)
    texts[pl.ds(0, ROWS), :] = (text_values * text_norm).astype(jnp.bfloat16)
    pl.semaphore_wait(barrier, len(peers))

    sent = []

    def send(source, target, arrival, device):
        copy = pltpu.make_async_remote_copy(
            src_ref=source, dst_ref=target, send_sem=send_sems.at[len(sent)], recv_sem=arrival,
            device_id=device, device_id_type=pl.DeviceIdType.MESH,
        )
        copy.start()
        sent.append(copy)

    def arrived(target, arrival):
        pltpu.make_async_copy(target, target, arrival).wait()

    def place(r, p, s):
        return texts.at[pl.ds((r * NY + p) * pair_rows + s * ROWS, ROWS), :]

    def forward(r):
        for p in range(NY - 1, 0, -1):
            send(place(r, 0, 0), place(r, p, 0), gather_recv.at[r, p], y_peer(moves[p]))
        send(place(r, 0, 0), place(r, 0, 1), gather_pair_recv.at[r, 0], sibling)

    def take(r, places):
        for p in places:
            if p > 0:
                arrived(place(r, p, 0), gather_recv.at[r, p])
                send(place(r, p, 0), place(r, p, 1), gather_pair_recv.at[r, p], sibling)

    def take_pair(r, places):
        for p in places:
            arrived(place(r, p, 1), gather_pair_recv.at[r, p])

    send(place(0, 0, 0), place(1, 0, 0), gather_recv.at[1, 0], opposite)
    forward(0)

    for load in loads[1:]:
        load.wait()

    @pl.loop(0, NX)
    def _(i):
        rows = pl.ds(pl.multiple_of(i * x_rows, x_rows), x_rows)
        values = image_in[rows, :].astype(jnp.float32)
        image_half[rows, :] = (values * inverse_norms(values)).astype(jnp.bfloat16)

    scale_row = jnp.exp(jnp.full((1, image_half.shape[0]), scale_in[0], jnp.float32))
    bias = bias_in[0]
    some = NY // 2
    some_rows = some * pair_rows

    def coefficients(r, half):
        start = (2 * r + half) * some_rows
        logits = lax.dot_general(
            texts[pl.ds(start, some_rows), :], image_half[...], (((1,), (1,)), ((), ())),
            preferred_element_type=jnp.float32,
        ) * scale_row + bias
        if start == 0:
            text_ids = lax.broadcasted_iota(jnp.int32, logits.shape, 0)
            image_ids = lax.broadcasted_iota(jnp.int32, logits.shape, 1)
            same = jnp.logical_and(text_ids < ROWS, image_ids == text_ids + group * ROWS)
            sign = jnp.where(same, jnp.float32(1.0), jnp.float32(-1.0))
            values = -sign / (1.0 + jnp.exp(sign * logits))
        else:
            values = 1.0 / (1.0 + jnp.exp(-logits))
        coef_text[pl.ds(start, some_rows), :] = values.astype(jnp.bfloat16)
        coef[:, pl.ds(start, some_rows)] = values.T.astype(jnp.bfloat16)

    def text_share(r, half):
        share = jnp.dot(
            coef_text[pl.ds((2 * r + half) * some_rows, some_rows), :], image_half[...],
            preferred_element_type=jnp.float32,
        )
        for i in range(some):
            base = i * pair_rows
            text_own[r, half * some + i] = share[base : base + ROWS]
            pair_send[r, half, i] = share[base + ROWS : base + pair_rows].astype(jnp.bfloat16)
        send(pair_send.at[r, half], pair_recv.at[r, half], pair_sem.at[r, half], sibling)

    def pair_sum(r):
        for half in range(1, -1, -1):
            arrived(pair_recv.at[r, half], pair_sem.at[r, half])
            for i in range(some - 1, -1, -1):
                p = half * some + i
                both = text_own[r, p] + pair_recv[r, half, i].astype(jnp.float32)
                if p == 0:
                    text_own[r, 0] = both
                else:
                    y_send[r, p] = both.astype(jnp.bfloat16)

    def y_sends(r):
        for p in range(NY - 1, 0, -1):
            send(y_send.at[r, p], y_recv.at[r, p], y_sem.at[r, p], y_peer(-moves[p]))

    def y_sum(r):
        total = text_own[r, 0]
        for p in range(1, NY):
            arrived(y_recv.at[r, p], y_sem.at[r, p])
            total += y_recv[r, p].astype(jnp.float32)
        return total

    def image_share(k):
        rows = pl.ds(pl.multiple_of(lax.rem(x + k, NX) * x_rows, x_rows), x_rows)
        share = jnp.dot(coef[rows, :], texts[...], preferred_element_type=jnp.float32)
        if k == 0:
            x_own[...] = share
        else:
            x_send[k] = share.astype(jnp.bfloat16)

    def piece_rows(j):
        return pl.ds(pl.multiple_of(lax.rem(z_pair + j, pairs) * pair_rows, pair_rows), pair_rows)

    def x_sends(j, k):
        send(x_send.at[k, piece_rows(j), :], x_recv.at[j, k], x_sem.at[j, k], x_peer(k))

    def x_sum(j):
        total = x_own[piece_rows(j), :]
        for k in range(1, NX):
            arrived(x_recv.at[j, k], x_sem.at[j, k])
            total += x_recv[j, k].astype(jnp.float32)
        z_own[j] = total
        theirs = pl.ds(pl.multiple_of((1 - z_side) * ROWS, ROWS), ROWS)
        near_send[j] = z_own[j, theirs, :].astype(jnp.bfloat16)
        send(near_send.at[j], near_recv.at[j], near_sem.at[j], near)

    def near_sum(j):
        arrived(near_recv.at[j], near_sem.at[j])
        ours = pl.ds(pl.multiple_of(z_side * ROWS, ROWS), ROWS)
        return z_own[j, ours, :] + near_recv[j].astype(jnp.float32)

    def far_sends(j):
        far_send[j] = near_sum(j).astype(jnp.bfloat16)
        send(far_send.at[j], far_recv.at[j], far_sem.at[j], far_peer(j))

    first, second = range(some), range(some, NY)
    take(0, range(NY))
    arrived(place(1, 0, 0), gather_recv.at[1, 0])
    forward(1)
    for half, places in enumerate((first, second)):
        take_pair(0, places)
        coefficients(0, half)
    text_share(0, 0)
    text_share(0, 1)
    take(1, first)
    take(1, second[: some // 2])
    take_pair(1, first)
    coefficients(1, 0)
    text_share(1, 0)
    pair_sum(0)
    take(1, second[some // 2 :])
    take_pair(1, second)
    coefficients(1, 1)
    text_share(1, 1)

    x_order = [2, 1, 3] if NX == 4 else list(range(1, NX))
    j_order = [2, 1, 3, 0] if pairs == 4 else list(range(pairs - 1, -1, -1))
    image_share(x_order[0])
    x_sends(j_order[0], x_order[0])
    pair_sum(1)
    y_sends(1)
    for k in x_order[1:]:
        image_share(k)
        x_sends(j_order[0], k)
    for j in j_order[1:]:
        for k in x_order:
            x_sends(j, k)
    y_sends(0)
    image_share(0)

    x_sum(j_order[0])
    hi_send[...] = y_sum(1).astype(jnp.bfloat16)
    send(hi_send, hi_recv, hi_sem, opposite)
    for before, j in zip(j_order, j_order[1:]):
        x_sum(j)
        far_sends(before)
    text_total = y_sum(0)
    total = near_sum(0)
    for j in j_order[:-1]:
        arrived(far_recv.at[j], far_sem.at[j])
        total += far_recv[j].astype(jnp.float32)
    scale = jnp.exp(jnp.full((1, image_in.shape[1]), scale_in[0], jnp.float32))
    own = image_in[pl.ds(pl.multiple_of(group * ROWS, ROWS), ROWS), :].astype(jnp.float32)
    own_norm = inverse_norms(own)
    image_out[...] = norm_backward(own * own_norm, total * scale, own_norm)

    arrived(hi_recv, hi_sem)
    text_total += hi_recv[...].astype(jnp.float32)
    text_out[...] = norm_backward(text_values * text_norm, text_total * scale, text_norm)

    for copy in sent:
        copy.wait_send()


def body(image_embeds, text_embeds, scale_logarithm, logit_bias):
    images, width = image_embeds.shape
    count = NY * 4 * ROWS
    x_rows = NZ * ROWS
    pairs = NZ // 2
    sends = 1 + 4 * NY - 2 + 4 + 2 * NY - 2 + pairs * (NX - 1) + 2 * pairs - 1 + 1 + 2
    dma = pltpu.SemaphoreType.DMA

    def half(*shape):
        return pltpu.VMEM((*shape, width), jnp.bfloat16)

    def full(*shape):
        return pltpu.VMEM((*shape, width), jnp.float32)

    return pl.pallas_call(
        kernel,
        out_shape=[jax.ShapeDtypeStruct((ROWS, width), jnp.float32)] * 2,
        in_specs=[pl.BlockSpec(memory_space=pl.ANY)] * 4,
        out_specs=[pl.BlockSpec(memory_space=pltpu.VMEM)] * 2,
        scratch_shapes=[
            half(images),
            half(ROWS),
            pltpu.SMEM((1,), jnp.float32),
            pltpu.SMEM((1,), jnp.float32),
            half(images),
            half(count),
            pltpu.VMEM((images, count), jnp.bfloat16),
            pltpu.VMEM((count, images), jnp.bfloat16),
            half(2, 2, NY // 2, ROWS),
            half(2, 2, NY // 2, ROWS),
            full(2, NY, ROWS),
            half(2, NY, ROWS),
            half(2, NY, ROWS),
            half(ROWS),
            half(ROWS),
            full(x_rows),
            half(NX, x_rows),
            half(pairs, NX, 2 * ROWS),
            full(pairs, 2 * ROWS),
            half(pairs, ROWS),
            half(pairs, ROWS),
            half(pairs, ROWS),
            half(pairs, ROWS),
            dma((4,)),
            dma((2, NY)),
            dma((2, NY)),
            dma((2, 2)),
            dma((2, NY)),
            dma,
            dma((pairs, NX)),
            dma((pairs,)),
            dma((pairs,)),
            dma((sends,)),
        ],
        compiler_params=pltpu.CompilerParams(
            collective_id=0, has_side_effects=True, vmem_limit_bytes=VMEM_BYTES
        ),
        cost_estimate=pl.CostEstimate(
            flops=6 * images * count * width, bytes_accessed=4 * images * width,
            transcendentals=images * count,
        ),
    )(image_embeds, text_embeds, scale_logarithm, logit_bias)


def solution(mesh):
    return jax.shard_map(
        body,
        mesh=mesh,
        in_specs=(P("dp", None), P(("dp", "group"), None), P(), P()),
        out_specs=(P(("dp", "group"), None), P(("dp", "group"), None)),
        check_vma=False,
    )
```

time: 83.5 us -> 74.7 us (0.89)
  the two profiles are of different devices: /device:TPU:128 before, /device:TPU:11 now
where the time goes in v2:
time: 74.7 us; the launch traced here: 74.4 us
  Pallas kernels  69.5 us (93%)
  local copies, waits for them, and re-layouts  3.04 us (4%)
  between operations  1.93 us (3%)
    pallas_call x1, Pallas kernels, body(): pl.pallas_call(kernel, out_shape=[jax.ShapeDtypeStruct((ROWS, width), jnp...  69.5 us
    unnamed x2, local copies, waits for them, and re-layouts  3.04 us

profile of v2, /device:TPU:11, one launch (start us, length us, event | category | flops | bytes accessed | tf_op | source)
XLA Modules:
  0.0 74.4 jit_solution(16122828364518330083)
XLA Ops:
  1.9 69.5 %shard_map.59 = (f32[16,1152]{1,0:T(8,128)}, f32[16,1152]{1,0:T(8,128)}) custom-call(bf16[512,1152]{1,0:T(8,128)(2,1)} %image_hbm.1, bf16[16,1152]{1,0:T(8,128)(2,1)} %text_hbm.1, f32[1]{0:T(128)S(6)} %copy.8.scale_hbm, f32[1]{0:T(128)S(6)} %copy.9.bias_hbm), custom_call_target="tpu_custom_call" | custom-call | flops 1811939328 | bytes 2359296 | tf_op jit(solution)/shard_map/pallas_call | solution.py:295
  71.4 1.5 %copy.10 = f32[16,1152]{1,0:T(8,128)} copy(f32[16,1152]{1,0:T(8,128)} %get-tuple-element.4) | data formatting | bytes 147456
  72.9 1.5 %copy.11 = f32[16,1152]{1,0:T(8,128)} copy(f32[16,1152]{1,0:T(8,128)} %get-tuple-element.5) | data formatting | bytes 147456

commit v3 on v2

--- a/solution.py
+++ b/solution.py
@@ -9,7 +9,7 @@
 NY = 8
 NZ = 8
 ROWS = 16
-VMEM_BYTES = 56 * 1024 * 1024
+VMEM_BYTES = 53 * 1024 * 1024 + 512 * 1024
 
 def offsets(count):
     found = [0]
@@ -31,8 +31,8 @@
     image_hbm, text_hbm, scale_hbm, bias_hbm, image_out, text_out,
     image_in, text_in, scale_in, bias_in, image_half, texts, coef, coef_text,
     pair_send, pair_recv, text_own, y_send, y_recv, hi_send, hi_recv,
-    x_own, x_send, x_recv, z_own, near_send, near_recv, far_send, far_recv,
-    in_sems, gather_recv, gather_pair_recv, pair_sem, y_sem, hi_sem, x_sem, near_sem, far_sem,
+    x_full, x_half, pass_send, pass_recv, x_recv, z_own, near_send, near_recv, far_send, far_recv,
+    in_sems, gather_recv, gather_pair_recv, pair_sem, y_sem, hi_sem, pass_sem, x_sem, near_sem, far_sem,
     send_sems,
 ):
     dp = lax.axis_index("dp")
@@ -62,8 +62,14 @@
     def x_peer(k):
         return (dp, lax.rem(x + k, NX) * NZ + z_lo)
 
+    def pair_at(j):
+        low, high = lax.rem(z_pair, 2), z_pair // 2
+        low = low if j % 2 == 0 else 1 - low
+        high = high if j < 2 else 1 - high
+        return high * 2 + low
+
     def far_peer(j):
-        return (dp, x * NZ + lax.rem(z_pair + j, pairs) * 2 + z_side)
+        return (dp, x * NZ + pair_at(j) * 2 + z_side)
 
     loads = [
         pltpu.make_async_copy(source, target, in_sems.at[i])
@@ -75,9 +81,9 @@
         load.start()
 
     peers = [opposite, sibling, near]
-    peers += [y_peer(move) for move in moves[1:]]
-    peers += [x_peer(k) for k in range(1, NX)]
-    peers += [far_peer(j) for j in range(1, pairs)]
+    peers += [y_peer(move) for move in moves[1:5]]
+    peers += [x_peer(1), x_peer(3)]
+    peers += [far_peer(1), far_peer(2)]
     barrier = pltpu.get_barrier_semaphore()
     for peer in peers:
         pl.semaphore_signal(barrier, inc=1, device_id=peer, device_id_type=pl.DeviceIdType.MESH)
@@ -86,41 +92,6 @@
     text_values = text_in[...].astype(jnp.float32)
     text_norm = inverse_norms(text_values)
     texts[pl.ds(0, ROWS), :] = (text_values * text_norm).astype(jnp.bfloat16)
-    pl.semaphore_wait(barrier, len(peers))
-
-    sent = []
-
-    def send(source, target, arrival, device):
-        copy = pltpu.make_async_remote_copy(
-            src_ref=source, dst_ref=target, send_sem=send_sems.at[len(sent)], recv_sem=arrival,
-            device_id=device, device_id_type=pl.DeviceIdType.MESH,
-        )
-        copy.start()
-        sent.append(copy)
-
-    def arrived(target, arrival):
-        pltpu.make_async_copy(target, target, arrival).wait()
-
-    def place(r, p, s):
-        return texts.at[pl.ds((r * NY + p) * pair_rows + s * ROWS, ROWS), :]
-
-    def forward(r):
-        for p in range(NY - 1, 0, -1):
-            send(place(r, 0, 0), place(r, p, 0), gather_recv.at[r, p], y_peer(moves[p]))
-        send(place(r, 0, 0), place(r, 0, 1), gather_pair_recv.at[r, 0], sibling)
-
-    def take(r, places):
-        for p in places:
-            if p > 0:
-                arrived(place(r, p, 0), gather_recv.at[r, p])
-                send(place(r, p, 0), place(r, p, 1), gather_pair_recv.at[r, p], sibling)
-
-    def take_pair(r, places):
-        for p in places:
-            arrived(place(r, p, 1), gather_pair_recv.at[r, p])
-
-    send(place(0, 0, 0), place(1, 0, 0), gather_recv.at[1, 0], opposite)
-    forward(0)
 
     for load in loads[1:]:
         load.wait()
@@ -130,6 +101,52 @@
         rows = pl.ds(pl.multiple_of(i * x_rows, x_rows), x_rows)
         values = image_in[rows, :].astype(jnp.float32)
         image_half[rows, :] = (values * inverse_norms(values)).astype(jnp.bfloat16)
+
+    pl.semaphore_wait(barrier, len(peers))
+
+    started, pending = [], {}
+
+    def send(source, target, arrival, device):
+        copy = pltpu.make_async_remote_copy(
+            src_ref=source, dst_ref=target, send_sem=send_sems.at[len(started)], recv_sem=arrival,
+            device_id=device, device_id_type=pl.DeviceIdType.MESH,
+        )
+        copy.start()
+        pending[len(started)] = copy
+        started.append(copy)
+        return len(started) - 1
+
+    def arrived(target, arrival):
+        pltpu.make_async_copy(target, target, arrival).wait()
+
+    def place(r, p, s):
+        start = (r * NY + p) * pair_rows + s * ROWS
+        return texts.at[pl.ds(start if isinstance(start, int) else pl.multiple_of(start, ROWS), ROWS), :]
+
+    def gather_send(r, source, target, move):
+        send(place(r, source, 0), place(r, target, 0), gather_recv.at[r, target], y_peer(move))
+
+    def forward(r):
+        for p in (3, 4, 1, 2):
+            gather_send(r, 0, p, moves[p])
+        send(place(r, 0, 0), place(r, 0, 1), gather_pair_recv.at[r, 0], sibling)
+
+    def take(r, places):
+        for p in places:
+            arrived(place(r, p, 0), gather_recv.at[r, p])
+            if p == 3:
+                gather_send(r, 3, 5, 1)
+            elif p == 4:
+                gather_send(r, 4, 6, -1)
+                gather_send(r, 3 + core, 7, 2 - 4 * core)
+            send(place(r, p, 0), place(r, p, 1), gather_pair_recv.at[r, p], sibling)
+
+    def take_pair(r, places):
+        for p in places:
+            arrived(place(r, p, 1), gather_pair_recv.at[r, p])
+
+    send(place(0, 0, 0), place(1, 0, 0), gather_recv.at[1, 0], opposite)
+    forward(0)
 
     scale_row = jnp.exp(jnp.full((1, image_half.shape[0]), scale_in[0], jnp.float32))
     bias = bias_in[0]
@@ -170,18 +187,34 @@
             for i in range(some - 1, -1, -1):
                 p = half * some + i
                 both = text_own[r, p] + pair_recv[r, half, i].astype(jnp.float32)
-                if p == 0:
-                    text_own[r, 0] = both
+                if p in (0, 3, 4):
+                    text_own[r, p] = both
                 else:
                     y_send[r, p] = both.astype(jnp.bfloat16)
 
-    def y_sends(r):
-        for p in range(NY - 1, 0, -1):
-            send(y_send.at[r, p], y_recv.at[r, p], y_sem.at[r, p], y_peer(-moves[p]))
+    def y_send_to(r, p, move):
+        send(y_send.at[r, p], y_recv.at[r, p], y_sem.at[r, p], y_peer(move))
+
+    def y_first(r):
+        y_send_to(r, 7, 2 - 4 * core)
+        y_send_to(r, 6, 1)
+        y_send_to(r, 5, -1)
+        y_send_to(r, 2, 1)
+        y_send_to(r, 1, -1)
+
+    def y_pass(r):
+        for p in (5, 6, 7):
+            arrived(y_recv.at[r, p], y_sem.at[r, p])
+        last = y_recv[r, 7].astype(jnp.float32)
+        for p in (3, 4):
+            both = text_own[r, p] + y_recv[r, p + 2].astype(jnp.float32)
+            both += jnp.where(core == 4 - p, last, jnp.zeros_like(last))
+            y_send[r, p] = both.astype(jnp.bfloat16)
+            y_send_to(r, p, -moves[p])
 
     def y_sum(r):
         total = text_own[r, 0]
-        for p in range(1, NY):
+        for p in range(1, 5):
             arrived(y_recv.at[r, p], y_sem.at[r, p])
             total += y_recv[r, p].astype(jnp.float32)
         return total
@@ -189,80 +222,119 @@
     def image_share(k):
         rows = pl.ds(pl.multiple_of(lax.rem(x + k, NX) * x_rows, x_rows), x_rows)
         share = jnp.dot(coef[rows, :], texts[...], preferred_element_type=jnp.float32)
-        if k == 0:
-            x_own[...] = share
-        else:
-            x_send[k] = share.astype(jnp.bfloat16)
-
-    def piece_rows(j):
-        return pl.ds(pl.multiple_of(lax.rem(z_pair + j, pairs) * pair_rows, pair_rows), pair_rows)
-
-    def x_sends(j, k):
-        send(x_send.at[k, piece_rows(j), :], x_recv.at[j, k], x_sem.at[j, k], x_peer(k))
+        if k != 2:
+            x_full[k] = share
+        if k != 0:
+            x_half[k] = share.astype(jnp.bfloat16)
+
+    def side_rows(j, side):
+        start = (pair_at(j) * 2 + side) * ROWS
+        return pl.ds(pl.multiple_of(start, ROWS), ROWS)
+
+    def pass_sends(j):
+        for way in range(2):
+            send(
+                x_half.at[2, side_rows(j, way), :], pass_recv.at[j, way], pass_sem.at[j, way],
+                x_peer(1 + 2 * way),
+            )
+
+    going = [[] for _ in range(pairs)]
+
+    def x_sends(j):
+        for way in range(2):
+            going[j].append(send(
+                x_half.at[1 + 2 * way, side_rows(j, 1 - way), :], x_recv.at[j, way, 1 - way],
+                x_sem.at[j, way, 1 - way], x_peer(1 + 2 * way),
+            ))
+        for way in range(2):
+            arrived(pass_recv.at[j, way], pass_sem.at[j, way])
+            both = x_full[1 + 2 * way, side_rows(j, way), :] + pass_recv[j, way].astype(jnp.float32)
+            pass_send[j, way] = both.astype(jnp.bfloat16)
+            going[j].append(send(
+                pass_send.at[j, way], x_recv.at[j, way, way], x_sem.at[j, way, way],
+                x_peer(1 + 2 * way),
+            ))
+
+    def settle(j):
+        for index in going[j]:
+            pending.pop(index).wait_send()
 
     def x_sum(j):
-        total = x_own[piece_rows(j), :]
-        for k in range(1, NX):
-            arrived(x_recv.at[j, k], x_sem.at[j, k])
-            total += x_recv[j, k].astype(jnp.float32)
-        z_own[j] = total
-        theirs = pl.ds(pl.multiple_of((1 - z_side) * ROWS, ROWS), ROWS)
-        near_send[j] = z_own[j, theirs, :].astype(jnp.bfloat16)
+        for side in range(2):
+            total = x_full[0, side_rows(j, side), :]
+            for way in range(2):
+                arrived(x_recv.at[j, way, side], x_sem.at[j, way, side])
+                total += x_recv[j, way, side].astype(jnp.float32)
+            z_own[j, side] = total
+        near_send[j] = z_own[j, 1 - z_side].astype(jnp.bfloat16)
         send(near_send.at[j], near_recv.at[j], near_sem.at[j], near)
 
     def near_sum(j):
         arrived(near_recv.at[j], near_sem.at[j])
-        ours = pl.ds(pl.multiple_of(z_side * ROWS, ROWS), ROWS)
-        return z_own[j, ours, :] + near_recv[j].astype(jnp.float32)
-
-    def far_sends(j):
+        return z_own[j, z_side] + near_recv[j].astype(jnp.float32)
+
+    def middle_sends(j):
         far_send[j] = near_sum(j).astype(jnp.bfloat16)
-        send(far_send.at[j], far_recv.at[j], far_sem.at[j], far_peer(j))
+        send(far_send.at[j], far_recv.at[j], far_sem.at[j], far_peer(1))
+
+    def far_sends():
+        total = near_sum(2)
+        arrived(far_recv.at[3], far_sem.at[3])
+        far_send[2] = (total + far_recv[3].astype(jnp.float32)).astype(jnp.bfloat16)
+        send(far_send.at[2], far_recv.at[2], far_sem.at[2], far_peer(2))
 
     first, second = range(some), range(some, NY)
-    take(0, range(NY))
+    order = (3, 4, 1, 2)
+    rest = (5, 6, 7)
+    take(0, order)
     arrived(place(1, 0, 0), gather_recv.at[1, 0])
     forward(1)
+    take(0, rest)
+    take(1, order)
     for half, places in enumerate((first, second)):
         take_pair(0, places)
         coefficients(0, half)
-    text_share(0, 0)
-    text_share(0, 1)
-    take(1, first)
-    take(1, second[: some // 2])
+        text_share(0, half)
+    take(1, rest)
     take_pair(1, first)
     coefficients(1, 0)
     text_share(1, 0)
-    pair_sum(0)
-    take(1, second[some // 2 :])
     take_pair(1, second)
     coefficients(1, 1)
     text_share(1, 1)
 
-    x_order = [2, 1, 3] if NX == 4 else list(range(1, NX))
-    j_order = [2, 1, 3, 0] if pairs == 4 else list(range(pairs - 1, -1, -1))
-    image_share(x_order[0])
-    x_sends(j_order[0], x_order[0])
+    image_share(2)
+    pass_sends(3)
+    pass_sends(2)
     pair_sum(1)
-    y_sends(1)
-    for k in x_order[1:]:
-        image_share(k)
-        x_sends(j_order[0], k)
-    for j in j_order[1:]:
-        for k in x_order:
-            x_sends(j, k)
-    y_sends(0)
+    y_first(1)
+    image_share(1)
+    image_share(3)
+    x_sends(3)
+    pass_sends(1)
+    pair_sum(0)
     image_share(0)
-
-    x_sum(j_order[0])
+    y_pass(1)
+    x_sends(2)
+    settle(3)
+    pass_sends(0)
+    x_sends(1)
+    y_first(0)
+    x_sum(3)
+    settle(2)
+    x_sends(0)
     hi_send[...] = y_sum(1).astype(jnp.bfloat16)
     send(hi_send, hi_recv, hi_sem, opposite)
-    for before, j in zip(j_order, j_order[1:]):
-        x_sum(j)
-        far_sends(before)
+    x_sum(2)
+    middle_sends(3)
+    y_pass(0)
+    x_sum(1)
+    far_sends()
+    middle_sends(1)
+    x_sum(0)
     text_total = y_sum(0)
     total = near_sum(0)
-    for j in j_order[:-1]:
+    for j in (1, 2):
         arrived(far_recv.at[j], far_sem.at[j])
         total += far_recv[j].astype(jnp.float32)
     scale = jnp.exp(jnp.full((1, image_in.shape[1]), scale_in[0], jnp.float32))
@@ -274,7 +346,7 @@
     text_total += hi_recv[...].astype(jnp.float32)
     text_out[...] = norm_backward(text_values * text_norm, text_total * scale, text_norm)
 
-    for copy in sent:
+    for copy in pending.values():
         copy.wait_send()
 
 
@@ -283,7 +355,7 @@
     count = NY * 4 * ROWS
     x_rows = NZ * ROWS
     pairs = NZ // 2
-    sends = 1 + 4 * NY - 2 + 4 + 2 * NY - 2 + pairs * (NX - 1) + 2 * pairs - 1 + 1 + 2
+    sends = 1 + 4 * NY - 2 + 4 + 2 * NY - 2 + 6 * pairs + 2 * pairs - 1 + 1
     dma = pltpu.SemaphoreType.DMA
 
     def half(*shape):
@@ -313,10 +385,12 @@
             half(2, NY, ROWS),
             half(ROWS),
             half(ROWS),
-            full(x_rows),
+            full(NX, x_rows),
             half(NX, x_rows),
-            half(pairs, NX, 2 * ROWS),
-            full(pairs, 2 * ROWS),
+            half(pairs, 2, ROWS),
+            half(pairs, 2, ROWS),
+            half(pairs, 2, 2, ROWS),
+            full(pairs, 2, ROWS),
             half(pairs, ROWS),
             half(pairs, ROWS),
             half(pairs, ROWS),
@@ -327,7 +401,8 @@
             dma((2, 2)),
             dma((2, NY)),
             dma,
-            dma((pairs, NX)),
+            dma((pairs, 2)),
+            dma((pairs, 2, 2)),
             dma((pairs,)),
             dma((pairs,)),
             dma((sends,)),

time: 74.7 us -> 68.6 us (0.918)
  the two profiles are of different devices: /device:TPU:11 before, /device:TPU:8 now
where the time goes in v3:
time: 68.6 us; the launch traced here: 68.4 us
  Pallas kernels  64.4 us (94%)
  local copies, waits for them, and re-layouts  2.03 us (3%)
  between operations  1.94 us (3%)
    pallas_call x1, Pallas kernels, body(): pl.pallas_call(kernel, out_shape=[jax.ShapeDtypeStruct((ROWS, width), jnp...  64.4 us
    unnamed x4, local copies, waits for them, and re-layouts  2.03 us

profile of v3, /device:TPU:8, one launch (start us, length us, event | category | flops | bytes accessed | tf_op | source)
XLA Modules:
  0.0 68.4 jit_solution(12785141593420578337)
XLA Ops:
  1.9 0.0 copy-start
  1.9 0.8 %copy-done = bf16[16,1152]{1,0:T(8,128)(2,1)S(1)} copy-done((bf16[16,1152]{1,0:T(8,128)(2,1)S(1)}, bf16[16,1152]{1,0:T(8,128)(2,1)}, u32[]{:S(2)}) %copy-start) | copy-done | bytes 36888
  2.7 64.4 %shard_map.59 = (f32[16,1152]{1,0:T(8,128)S(1)}, f32[16,1152]{1,0:T(8,128)S(1)}) custom-call(bf16[512,1152]{1,0:T(8,128)(2,1)} %image_hbm.1, bf16[16,1152]{1,0:T(8,128)(2,1)S(1)} %copy-done, f32[1]{0:T(128)S(6)} %copy.8.scale_hbm, f32[1]{0:T(128)S(6)} %copy.9.bias_hbm), custom_call_target="tpu_custom_call" | custom-call | flops 1811939328 | bytes 2359296 | tf_op jit(solution)/shard_map/pallas_call | solution.py:367
  67.1 0.6 copy.10
  67.7 0.6 copy.11
Async XLA Ops:
  1.9 0.8 %copy-start = (bf16[16,1152]{1,0:T(8,128)(2,1)S(1)}, bf16[16,1152]{1,0:T(8,128)(2,1)}, u32[]{:S(2)}) copy-start(bf16[16,1152]{1,0:T(8,128)(2,1)} %text_hbm.1) | copy-start | bytes 110596

commit v4 on v3

--- a/solution.py
+++ b/solution.py
@@ -71,6 +71,14 @@
     def far_peer(j):
         return (dp, x * NZ + pair_at(j) * 2 + z_side)
 
+    peers = [opposite, sibling, near]
+    peers += [y_peer(move) for move in moves[1:5]]
+    peers += [x_peer(1), x_peer(3)]
+    peers += [far_peer(1), far_peer(2)]
+    barrier = pltpu.get_barrier_semaphore()
+    for peer in peers:
+        pl.semaphore_signal(barrier, inc=1, device_id=peer, device_id_type=pl.DeviceIdType.MESH)
+
     loads = [
         pltpu.make_async_copy(source, target, in_sems.at[i])
         for i, (source, target) in enumerate(
@@ -80,14 +88,6 @@
     for load in loads:
         load.start()
 
-    peers = [opposite, sibling, near]
-    peers += [y_peer(move) for move in moves[1:5]]
-    peers += [x_peer(1), x_peer(3)]
-    peers += [far_peer(1), far_peer(2)]
-    barrier = pltpu.get_barrier_semaphore()
-    for peer in peers:
-        pl.semaphore_signal(barrier, inc=1, device_id=peer, device_id_type=pl.DeviceIdType.MESH)
-
     loads[0].wait()
     text_values = text_in[...].astype(jnp.float32)
     text_norm = inverse_norms(text_values)
@@ -104,17 +104,15 @@
 
     pl.semaphore_wait(barrier, len(peers))
 
-    started, pending = [], {}
+    sent = []
 
     def send(source, target, arrival, device):
         copy = pltpu.make_async_remote_copy(
-            src_ref=source, dst_ref=target, send_sem=send_sems.at[len(started)], recv_sem=arrival,
+            src_ref=source, dst_ref=target, send_sem=send_sems.at[len(sent)], recv_sem=arrival,
             device_id=device, device_id_type=pl.DeviceIdType.MESH,
         )
         copy.start()
-        pending[len(started)] = copy
-        started.append(copy)
-        return len(started) - 1
+        sent.append(copy)
 
     def arrived(target, arrival):
         pltpu.make_async_copy(target, target, arrival).wait()
@@ -238,26 +236,22 @@
                 x_peer(1 + 2 * way),
             )
 
-    going = [[] for _ in range(pairs)]
-
     def x_sends(j):
         for way in range(2):
-            going[j].append(send(
+            send(
                 x_half.at[1 + 2 * way, side_rows(j, 1 - way), :], x_recv.at[j, way, 1 - way],
                 x_sem.at[j, way, 1 - way], x_peer(1 + 2 * way),
-            ))
+            )
+
+    def pass_on(j):
         for way in range(2):
             arrived(pass_recv.at[j, way], pass_sem.at[j, way])
             both = x_full[1 + 2 * way, side_rows(j, way), :] + pass_recv[j, way].astype(jnp.float32)
             pass_send[j, way] = both.astype(jnp.bfloat16)
-            going[j].append(send(
+            send(
                 pass_send.at[j, way], x_recv.at[j, way, way], x_sem.at[j, way, way],
                 x_peer(1 + 2 * way),
-            ))
-
-    def settle(j):
-        for index in going[j]:
-            pending.pop(index).wait_send()
+            )
 
     def x_sum(j):
         for side in range(2):
@@ -301,34 +295,36 @@
     text_share(1, 0)
     take_pair(1, second)
     coefficients(1, 1)
-    text_share(1, 1)
 
     image_share(2)
     pass_sends(3)
-    pass_sends(2)
-    pair_sum(1)
-    y_first(1)
     image_share(1)
     image_share(3)
     x_sends(3)
+    text_share(1, 1)
+    pass_sends(2)
+    pass_on(3)
+    pair_sum(1)
+    y_first(1)
+    x_sends(2)
+    image_share(0)
+    pair_sum(0)
     pass_sends(1)
-    pair_sum(0)
-    image_share(0)
+    pass_on(2)
+    x_sends(1)
+    pass_sends(0)
     y_pass(1)
-    x_sends(2)
-    settle(3)
-    pass_sends(0)
-    x_sends(1)
+    x_sum(3)
+    pass_on(1)
+    x_sends(0)
     y_first(0)
-    x_sum(3)
-    settle(2)
-    x_sends(0)
+    pass_on(0)
+    middle_sends(3)
+    x_sum(2)
     hi_send[...] = y_sum(1).astype(jnp.bfloat16)
     send(hi_send, hi_recv, hi_sem, opposite)
-    x_sum(2)
-    middle_sends(3)
+    x_sum(1)
     y_pass(0)
-    x_sum(1)
     far_sends()
     middle_sends(1)
     x_sum(0)
@@ -346,7 +342,7 @@
     text_total += hi_recv[...].astype(jnp.float32)
     text_out[...] = norm_backward(text_values * text_norm, text_total * scale, text_norm)
 
-    for copy in pending.values():
+    for copy in sent:
         copy.wait_send()
 
 

time: 68.6 us -> 69.2 us (level)
  no operation moved by 1% of the time
where the time goes in v4:
time: 69.2 us; the launch traced here: 68.9 us
  Pallas kernels  65 us (94%)
  local copies, waits for them, and re-layouts  2.03 us (3%)
  between operations  1.94 us (3%)
    pallas_call x1, Pallas kernels, body(): pl.pallas_call(kernel, out_shape=[jax.ShapeDtypeStruct((ROWS, width), jnp...  65 us
    unnamed x4, local copies, waits for them, and re-layouts  2.03 us

profile of v4, /device:TPU:8, one launch (start us, length us, event | category | flops | bytes accessed | tf_op | source)
XLA Modules:
  0.0 68.9 jit_solution(17819638341809343682)
XLA Ops:
  1.9 0.0 copy-start
  1.9 0.8 %copy-done = bf16[16,1152]{1,0:T(8,128)(2,1)S(1)} copy-done((bf16[16,1152]{1,0:T(8,128)(2,1)S(1)}, bf16[16,1152]{1,0:T(8,128)(2,1)}, u32[]{:S(2)}) %copy-start) | copy-done | bytes 36888
  2.7 65.0 %shard_map.59 = (f32[16,1152]{1,0:T(8,128)S(1)}, f32[16,1152]{1,0:T(8,128)S(1)}) custom-call(bf16[512,1152]{1,0:T(8,128)(2,1)} %image_hbm.1, bf16[16,1152]{1,0:T(8,128)(2,1)S(1)} %copy-done, f32[1]{0:T(128)S(6)} %copy.8.scale_hbm, f32[1]{0:T(128)S(6)} %copy.9.bias_hbm), custom_call_target="tpu_custom_call" | custom-call | flops 1811939328 | bytes 2359296 | tf_op jit(solution)/shard_map/pallas_call | solution.py:363
  67.7 0.6 copy.10
  68.3 0.6 copy.11
Async XLA Ops:
  1.9 0.8 %copy-start = (bf16[16,1152]{1,0:T(8,128)(2,1)S(1)}, bf16[16,1152]{1,0:T(8,128)(2,1)}, u32[]{:S(2)}) copy-start(bf16[16,1152]{1,0:T(8,128)(2,1)} %text_hbm.1) | copy-start | bytes 110596

commit v5 on v3

--- a/solution.py
+++ b/solution.py
@@ -71,6 +71,14 @@
     def far_peer(j):
         return (dp, x * NZ + pair_at(j) * 2 + z_side)
 
+    peers = [opposite, sibling, near]
+    peers += [y_peer(move) for move in moves[1:]]
+    peers += [x_peer(1), x_peer(3)]
+    peers += [far_peer(1), far_peer(2)]
+    barrier = pltpu.get_barrier_semaphore()
+    for peer in peers:
+        pl.semaphore_signal(barrier, inc=1, device_id=peer, device_id_type=pl.DeviceIdType.MESH)
+
     loads = [
         pltpu.make_async_copy(source, target, in_sems.at[i])
         for i, (source, target) in enumerate(
@@ -79,14 +87,6 @@
     ]
     for load in loads:
         load.start()
-
-    peers = [opposite, sibling, near]
-    peers += [y_peer(move) for move in moves[1:5]]
-    peers += [x_peer(1), x_peer(3)]
-    peers += [far_peer(1), far_peer(2)]
-    barrier = pltpu.get_barrier_semaphore()
-    for peer in peers:
-        pl.semaphore_signal(barrier, inc=1, device_id=peer, device_id_type=pl.DeviceIdType.MESH)
 
     loads[0].wait()
     text_values = text_in[...].astype(jnp.float32)
@@ -127,16 +127,16 @@
         send(place(r, source, 0), place(r, target, 0), gather_recv.at[r, target], y_peer(move))
 
     def forward(r):
-        for p in (3, 4, 1, 2):
+        for p in (3, 4, 1, 2) if r == 0 else range(NY - 1, 0, -1):
             gather_send(r, 0, p, moves[p])
         send(place(r, 0, 0), place(r, 0, 1), gather_pair_recv.at[r, 0], sibling)
 
     def take(r, places):
         for p in places:
             arrived(place(r, p, 0), gather_recv.at[r, p])
-            if p == 3:
+            if r == 0 and p == 3:
                 gather_send(r, 3, 5, 1)
-            elif p == 4:
+            elif r == 0 and p == 4:
                 gather_send(r, 4, 6, -1)
                 gather_send(r, 3 + core, 7, 2 - 4 * core)
             send(place(r, p, 0), place(r, p, 1), gather_pair_recv.at[r, p], sibling)
@@ -290,12 +290,11 @@
     arrived(place(1, 0, 0), gather_recv.at[1, 0])
     forward(1)
     take(0, rest)
-    take(1, order)
     for half, places in enumerate((first, second)):
         take_pair(0, places)
         coefficients(0, half)
         text_share(0, half)
-    take(1, rest)
+    take(1, range(1, NY))
     take_pair(1, first)
     coefficients(1, 0)
     text_share(1, 0)

time: 68.6 us -> 68.9 us (level)
  no operation moved by 1% of the time
where the time goes in v5:
time: 68.9 us; the launch traced here: 68.6 us
  Pallas kernels  64.6 us (94%)
  local copies, waits for them, and re-layouts  2.03 us (3%)
  between operations  1.94 us (3%)
    pallas_call x1, Pallas kernels, body(): pl.pallas_call(kernel, out_shape=[jax.ShapeDtypeStruct((ROWS, width), jnp...  64.6 us
    unnamed x4, local copies, waits for them, and re-layouts  2.03 us

profile of v5, /device:TPU:8, one launch (start us, length us, event | category | flops | bytes accessed | tf_op | source)
XLA Modules:
  0.0 68.6 jit_solution(608750558602661292)
XLA Ops:
  1.9 0.0 copy-start
  1.9 0.8 %copy-done = bf16[16,1152]{1,0:T(8,128)(2,1)S(1)} copy-done((bf16[16,1152]{1,0:T(8,128)(2,1)S(1)}, bf16[16,1152]{1,0:T(8,128)(2,1)}, u32[]{:S(2)}) %copy-start) | copy-done | bytes 36888
  2.7 64.6 %shard_map.59 = (f32[16,1152]{1,0:T(8,128)S(1)}, f32[16,1152]{1,0:T(8,128)S(1)}) custom-call(bf16[512,1152]{1,0:T(8,128)(2,1)} %image_hbm.1, bf16[16,1152]{1,0:T(8,128)(2,1)S(1)} %copy-done, f32[1]{0:T(128)S(6)} %copy.8.scale_hbm, f32[1]{0:T(128)S(6)} %copy.9.bias_hbm), custom_call_target="tpu_custom_call" | custom-call | flops 1811939328 | bytes 2359296 | tf_op jit(solution)/shard_map/pallas_call | solution.py:366
  67.3 0.6 copy.10
  68.0 0.6 copy.11
Async XLA Ops:
  1.9 0.8 %copy-start = (bf16[16,1152]{1,0:T(8,128)(2,1)S(1)}, bf16[16,1152]{1,0:T(8,128)(2,1)}, u32[]{:S(2)}) copy-start(bf16[16,1152]{1,0:T(8,128)(2,1)} %text_hbm.1) | copy-start | bytes 110596

commit v6 on v5

--- a/solution.py
+++ b/solution.py
@@ -322,10 +322,10 @@
     x_sum(3)
     settle(2)
     x_sends(0)
+    middle_sends(3)
     hi_send[...] = y_sum(1).astype(jnp.bfloat16)
     send(hi_send, hi_recv, hi_sem, opposite)
     x_sum(2)
-    middle_sends(3)
     y_pass(0)
     x_sum(1)
     far_sends()

time: 68.9 us -> 69.8 us (1.013)
  Pallas kernels: 64.6 us -> 65.6 us
    pallas_call x1, Pallas kernels: 64.6 us -> 65.6 us  [body(): pl.pallas_call(kernel, out_shape=[jax.ShapeDtypeStruct((ROWS, width), jnp...]
where the time goes in v6:
time: 69.8 us; the launch traced here: 69.5 us
  Pallas kernels  65.6 us (94%)
  local copies, waits for them, and re-layouts  2.03 us (3%)
  between operations  1.94 us (3%)
    pallas_call x1, Pallas kernels, body(): pl.pallas_call(kernel, out_shape=[jax.ShapeDtypeStruct((ROWS, width), jnp...  65.6 us
    unnamed x4, local copies, waits for them, and re-layouts  2.03 us

profile of v6, /device:TPU:8, one launch (start us, length us, event | category | flops | bytes accessed | tf_op | source)
XLA Modules:
  0.0 69.5 jit_solution(7991717855306683975)
XLA Ops:
  1.9 0.0 copy-start
  1.9 0.8 %copy-done = bf16[16,1152]{1,0:T(8,128)(2,1)S(1)} copy-done((bf16[16,1152]{1,0:T(8,128)(2,1)S(1)}, bf16[16,1152]{1,0:T(8,128)(2,1)}, u32[]{:S(2)}) %copy-start) | copy-done | bytes 36888
  2.7 65.6 %shard_map.59 = (f32[16,1152]{1,0:T(8,128)S(1)}, f32[16,1152]{1,0:T(8,128)S(1)}) custom-call(bf16[512,1152]{1,0:T(8,128)(2,1)} %image_hbm.1, bf16[16,1152]{1,0:T(8,128)(2,1)S(1)} %copy-done, f32[1]{0:T(128)S(6)} %copy.8.scale_hbm, f32[1]{0:T(128)S(6)} %copy.9.bias_hbm), custom_call_target="tpu_custom_call" | custom-call | flops 1811939328 | bytes 2359296 | tf_op jit(solution)/shard_map/pallas_call | solution.py:366
  68.3 0.6 copy.10
  68.9 0.6 copy.11
Async XLA Ops:
  1.9 0.8 %copy-start = (bf16[16,1152]{1,0:T(8,128)(2,1)S(1)}, bf16[16,1152]{1,0:T(8,128)(2,1)}, u32[]{:S(2)}) copy-start(bf16[16,1152]{1,0:T(8,128)(2,1)} %text_hbm.1) | copy-start | bytes 110596
